TPU v7x, 512 devices: a whole 4x4x16 slice. The times are simulated.
512 devices in a mesh: cuts: 2 (over y_lo), dp: 16 (over z), row: 4 (over y_hi, core), col: 4 (over x).
Axes of the slice: x: 4, y: 4 (y_hi: 2, y_lo: 2; y = y_hi * 2 + y_lo), z: 16, core: 2. Of those that a mesh axis runs over, the one named last changes fastest.
Arguments:
- tokens: bfloat16 [32768, 4096], P(('cuts', 'dp'), 'row'), may hold values from -6 to 6
- cotangent: bfloat16 [32768, 4096], P(('cuts', 'dp'), 'col'), may hold values from -0.03125 to 0.03125
- norm_gain: float32 [4096], P('row'), may hold values from 0.5 to 6
- row_prev: float32 [4, 1024], P('row', 'dp'), may hold values from 0.02 to 0.5
- col_prev: float32 [4096], P('col'), may hold values from 0.002 to 0.05
Outputs:
- update: float32 [4, 1024, 4096], P('row', 'dp', 'col')
- row_moment: float32 [4, 1024], P('row', 'dp')
- col_moment: float32 [4096], P('col')
All inputs are finite; a program needn't handle non-finite values.
Results may differ from a plain program's by a relative error of at most 0.0004.
Values sent between devices are 32-bit elements; how exact they have to be, the bound alone decides.
A program may use at most 64 MiB of HBM per device.

v0:
```python
import jax
import jax.numpy as jnp
from jax import lax
from jax.sharding import PartitionSpec as P

D = 4096
F = 4096
decay_rate = 0.975
epsilon_one = 1e-30
clip_level = 1.0


def gradient_rows(inputs, cotangent, gains):
    product = lax.dot_general(
        inputs, cotangent, (((0,), (0,)), ((), ())), preferred_element_type=jnp.float32
    )
    return product * gains[:, None]


def adafactor_step(gradient, rows_prev, cols_prev, down_columns, all_total):
    squares = gradient * gradient
    row_sum = lax.psum(jnp.sum(squares, axis=1), "col")
    col_sum = down_columns(jnp.sum(squares, axis=0))
    row_moment = decay_rate * rows_prev + (1.0 - decay_rate) * (row_sum / F + epsilon_one)
    col_moment = decay_rate * cols_prev + (1.0 - decay_rate) * (col_sum / D + epsilon_one)
    factor = row_moment[:, None] * col_moment[None, :]
    raw_update = gradient / jnp.sqrt(factor)
    total_squares = all_total(jnp.sum(raw_update * raw_update))
    clip_scale = jnp.maximum(1.0, jnp.sqrt(total_squares / (D * F)) / clip_level)
    return (raw_update / clip_scale, row_moment, col_moment)


def body(tokens, cotangent, norm_gain, row_prev, col_prev):
    slice_part = lax.psum_scatter(
        gradient_rows(tokens, cotangent, norm_gain), "dp", scatter_dimension=0, tiled=True
    )
    gradient = lax.psum(slice_part, "cuts")
    update, row_moment, col_moment = adafactor_step(
        gradient,
        row_prev[0],
        col_prev,
        lambda values: lax.psum(values, ("dp", "row")),
        lambda values: lax.psum(values, ("dp", "row", "col")),
    )
    return (update[None], row_moment[None], col_moment)


def solution(mesh):
    return jax.shard_map(
        body,
        mesh=mesh,
        in_specs=(
            P(("cuts", "dp"), "row"),
            P(("cuts", "dp"), "col"),
            P("row"),
            P("row", "dp"),
            P("col"),
        ),
        out_specs=(P("row", "dp", "col"), P("row", "dp"), P("col")),
        check_vma=False,
    )
```

profile of v0, /device:TPU:2, one launch (start us, length us, event | category | flops | bytes accessed | tf_op | source)
XLA Modules:
  0.0 946.8 jit_solution(15512773143829418762)
XLA Ops:
  7.2 0.0 copy-start
  7.2 0.0 reduce-scatter.2.cloned.1.call-start
  7.2 1.5 copy-done
  8.8 5.9 convolution_multiply_fusion
  14.7 0.0 copy-start.4
  14.7 0.0 copy-start.2
  14.7 0.0 reduce-scatter.2.cloned.1.call-update
  14.7 0.0 all-reduce.2.cloned.1.call-start
  14.7 84.2 %reduce-scatter.2.cloned.1.call-done = f32[64,1024]{1,0:T(8,128)} async-done(((f32[1024,1024]{1,0:T(8,128)}), f32[64,1024]{1,0:T(8,128)}) %reduce-scatter.2.cloned.1.call-update) | async-done | bytes 262160 | tf_op jit(solution)/shard_map/reduce_scatter | solution.py:34
  99.0 0.0 all-reduce.2.cloned.1.call-update
  99.0 45.7 %all-reduce.2.cloned.1.call-done = f32[64,1024]{1,0:T(8,128)} async-done(((f32[64,1024]{1,0:T(8,128)}), f32[64,1024]{1,0:T(8,128)}) %all-reduce.2.cloned.1.call-update) | async-done | bytes 262160 | tf_op jit(solution)/shard_map/psum | solution.py:37
  144.7 1.1 multiply_reduce_fusion.2
  145.8 8.6 psum.29
  154.4 132.2 %psum.30 = f32[1024]{0:T(1024)S(1)} all-reduce(f32[1024]{0:T(1024)S(1)} %get-tuple-element.4), channel_id=1, replica_groups=mesh['cuts'=2,'dp'=16,'row'=4,'col'=4] {'dp','row'}, use_global_device_ids=true, to_apply=%region_5.0 | all-reduce | flops 1024 | bytes 8192 | tf_op jit(solution)/shard_map/psum | solution.py:42
  286.6 0.0 copy-done.4
  286.6 0.0 copy-done.2
  286.6 0.0 copy-start.3
  286.7 0.0 copy-start.1
  286.7 1.7 multiply_reduce_fusion
  288.4 649.1 %psum.31 = f32[]{:T(128)} all-reduce(f32[]{:T(128)} %multiply_reduce_fusion), channel_id=1, replica_groups=mesh['cuts'=2,'dp'=16,'row'=4,'col'=4] {'dp','row','col'}, use_global_device_ids=true, to_apply=%region_7.0 | all-reduce | flops 1 | bytes 8 | tf_op jit(solution)/shard_map/psum | solution.py:43
  938.2 1.8 divide_bitcast_fusion
  939.9 0.0 copy-done.3
  939.9 0.0 copy-done.1
  (2 shorter events, 0.0 us)
Async XLA Ops:
  7.2 1.6 copy-start
  7.2 91.8 %reduce-scatter.2.cloned.1.call-start = ((), (), s32[]{:S(2)}) async-start(), calls=%async_computation.1 | async-start | bytes 4456448 | tf_op jit(solution)/shard_map/reduce_scatter | solution.py:34
  14.7 272.0 %copy-start.4 = (f32[1,64]{1,0:T(1,128)S(1)}, f32[1,64]{1,0:T(1,128)}, u32[]{:S(2)}) copy-start(f32[1,64]{1,0:T(1,128)} %param.8) | copy-start | bytes 772
  14.7 272.0 %copy-start.2 = (f32[1024]{0:T(1024)S(1)}, f32[1024]{0:T(1024)}, u32[]{:S(2)}) copy-start(f32[1024]{0:T(1024)} %param.9) | copy-start | bytes 12292
  14.7 130.0 %all-reduce.2.cloned.1.call-start = ((), (), s32[]{:S(2)}) async-start(), calls=%async_computation.2 | async-start | bytes 524288 | tf_op jit(solution)/shard_map/psum | solution.py:37
  286.6 653.3 %copy-start.3 = (f32[64]{0:T(128)}, f32[64]{0:T(128)S(1)}, u32[]{:S(2)}) copy-start(f32[64]{0:T(128)S(1)} %bitcast_add_fusion) | copy-start | bytes 772
  286.7 653.3 %copy-start.1 = (f32[1024]{0:T(1024)}, f32[1024]{0:T(1024)S(1)}, u32[]{:S(2)}) copy-start(f32[1024]{0:T(1024)S(1)} %multiply_add_fusion) | copy-start | bytes 12292
Sparse Core Ops, SparseCore 0:
  14.8 84.1 reduce-scatter.1
  101.8 42.8 all-reduce.1
where the time goes:
time: 947 us
  blocking collectives  790 us (83%)
  waiting for transfers between devices  130 us (14%)
  between operations  14.8 us (2%)
    psum x1, blocking collectives, body(): lax.psum(values, ('dp', 'row', 'col'))  649 us
    psum x1, blocking collectives, body(): lax.psum(values, ('dp', 'row'))  132 us
    reduce_scatter x1, waiting for transfers between devices, body(): lax.psum_scatter(gradient_rows(tokens, cotangent, norm_gain), 'dp', scatt...  84.2 us
    psum x1, waiting for transfers between devices, body(): gradient = lax.psum(slice_part, 'cuts')  45.7 us
  transfers between devices with their start and end apart: 2, of which 2 were waited for; matrix products, arithmetic and copies ran while one was open for 0% of the time, Pallas kernels for 0%

commit v1 on v0

--- a/solution.py
+++ b/solution.py
@@ -39,7 +39,7 @@
         gradient,
         row_prev[0],
         col_prev,
-        lambda values: lax.psum(values, ("dp", "row")),
+        lambda values: lax.psum(lax.psum(values, "row"), "dp"),
         lambda values: lax.psum(values, ("dp", "row", "col")),
     )
     return (update[None], row_moment[None], col_moment)

time: 947 us -> 854 us (0.902)
  blocking collectives: 790 us -> 696 us
    psum x1 -> x2, blocking collectives: 132 us -> 38.4 us  [the longest x1 31.3 us: body(): lax.psum(lax.psum(values, 'row'), 'dp')]
where the time goes in v1:
time: 854 us; the launch traced here: 853 us
  blocking collectives  696 us (81%)
  waiting for transfers between devices  130 us (15%)
  between operations  14.8 us (2%)
    psum x1, blocking collectives, body(): lax.psum(values, ('dp', 'row', 'col'))  649 us
    reduce_scatter x1, waiting for transfers between devices, body(): lax.psum_scatter(gradient_rows(tokens, cotangent, norm_gain), 'dp', scatt...  84.2 us
    psum x1, waiting for transfers between devices, body(): gradient = lax.psum(slice_part, 'cuts')  45.7 us
    psum x1, blocking collectives, body(): lax.psum(lax.psum(values, 'row'), 'dp')  31.3 us
  transfers between devices with their start and end apart: 2, of which 2 were waited for; matrix products, arithmetic and copies ran while one was open for 0% of the time, Pallas kernels for 0%

profile of v1, /device:TPU:2, one launch (start us, length us, event | category | flops | bytes accessed | tf_op | source)
XLA Modules:
  0.0 853.3 jit_solution(1096598771889961164)
XLA Ops:
  7.2 0.0 copy-start
  7.2 0.0 reduce-scatter.2.cloned.1.call-start
  7.2 1.5 copy-done
  8.8 5.9 convolution_multiply_fusion
  14.7 0.0 copy-start.4
  14.7 0.0 copy-start.2
  14.7 0.0 reduce-scatter.2.cloned.1.call-update
  14.7 0.0 all-reduce.2.cloned.1.call-start
  14.7 84.2 %reduce-scatter.2.cloned.1.call-done = f32[64,1024]{1,0:T(8,128)} async-done(((f32[1024,1024]{1,0:T(8,128)}), f32[64,1024]{1,0:T(8,128)}) %reduce-scatter.2.cloned.1.call-update) | async-done | bytes 262160 | tf_op jit(solution)/shard_map/reduce_scatter | solution.py:34
  99.0 0.0 all-reduce.2.cloned.1.call-update
  99.0 45.7 %all-reduce.2.cloned.1.call-done = f32[64,1024]{1,0:T(8,128)} async-done(((f32[64,1024]{1,0:T(8,128)}), f32[64,1024]{1,0:T(8,128)}) %all-reduce.2.cloned.1.call-update) | async-done | bytes 262160 | tf_op jit(solution)/shard_map/psum | solution.py:37
  144.7 1.1 multiply_reduce_fusion.2
  145.8 8.6 %psum.36 = f32[64]{0:T(128)S(1)} all-reduce(f32[64]{0:T(128)S(1)} %get-tuple-element.3), channel_id=1, replica_groups=mesh['cuts'=2,'dp'=16,'row'=4,'col'=4] {'col'}, use_global_device_ids=true, to_apply=%region_3.0 | all-reduce | flops 64 | bytes 512 | tf_op jit(solution)/shard_map/psum | solution.py:22
  154.4 7.2 psum.37
  161.6 31.3 %psum.38 = f32[1024]{0:T(1024)S(1)} all-reduce(f32[1024]{0:T(1024)S(1)} %psum.37), channel_id=1, replica_groups=mesh['cuts'=2,'dp'=16,'row'=4,'col'=4] {'dp'}, use_global_device_ids=true, to_apply=%region_6.0 | all-reduce | flops 1024 | bytes 8192 | tf_op jit(solution)/shard_map/psum | solution.py:42
  192.8 0.0 copy-done.4
  192.9 0.0 copy-done.2
  192.9 0.0 copy-start.3
  192.9 0.0 copy-start.1
  192.9 1.7 multiply_reduce_fusion
  194.6 649.4 %psum.39 = f32[]{:T(128)} all-reduce(f32[]{:T(128)} %multiply_reduce_fusion), channel_id=1, replica_groups=mesh['cuts'=2,'dp'=16,'row'=4,'col'=4] {'dp','row','col'}, use_global_device_ids=true, to_apply=%region_8.0 | all-reduce | flops 1 | bytes 8 | tf_op jit(solution)/shard_map/psum | solution.py:43
  844.7 1.8 divide_bitcast_fusion
  846.5 0.0 copy-done.3
  846.5 0.0 copy-done.1
  (2 shorter events, 0.0 us)
Async XLA Ops:
  7.2 1.6 copy-start
  7.2 91.8 %reduce-scatter.2.cloned.1.call-start = ((), (), s32[]{:S(2)}) async-start(), calls=%async_computation.1 | async-start | bytes 4456448 | tf_op jit(solution)/shard_map/reduce_scatter | solution.py:34
  14.7 178.2 %copy-start.4 = (f32[1,64]{1,0:T(1,128)S(1)}, f32[1,64]{1,0:T(1,128)}, u32[]{:S(2)}) copy-start(f32[1,64]{1,0:T(1,128)} %param.8) | copy-start | bytes 772
  14.7 178.2 %copy-start.2 = (f32[1024]{0:T(1024)S(1)}, f32[1024]{0:T(1024)}, u32[]{:S(2)}) copy-start(f32[1024]{0:T(1024)} %param.9) | copy-start | bytes 12292
  14.7 130.0 %all-reduce.2.cloned.1.call-start = ((), (), s32[]{:S(2)}) async-start(), calls=%async_computation.2 | async-start | bytes 524288 | tf_op jit(solution)/shard_map/psum | solution.py:37
  192.9 653.6 %copy-start.3 = (f32[64]{0:T(128)}, f32[64]{0:T(128)S(1)}, u32[]{:S(2)}) copy-start(f32[64]{0:T(128)S(1)} %bitcast_add_fusion) | copy-start | bytes 772
  192.9 653.6 %copy-start.1 = (f32[1024]{0:T(1024)}, f32[1024]{0:T(1024)S(1)}, u32[]{:S(2)}) copy-start(f32[1024]{0:T(1024)S(1)} %multiply_add_fusion) | copy-start | bytes 12292
Sparse Core Ops, SparseCore 0:
  14.8 84.1 reduce-scatter.1
  101.8 42.8 all-reduce.1

commit v2 on v0

--- a/solution.py
+++ b/solution.py
@@ -34,7 +34,7 @@
     slice_part = lax.psum_scatter(
         gradient_rows(tokens, cotangent, norm_gain), "dp", scatter_dimension=0, tiled=True
     )
-    gradient = lax.psum(slice_part, "cuts")
+    gradient = jnp.sum(lax.all_gather(slice_part, "cuts"), axis=0)
     update, row_moment, col_moment = adafactor_step(
         gradient,
         row_prev[0],

time: 947 us -> 903 us (0.954)
  waiting for transfers between devices: 130 us -> 84.3 us
    psum x1 -> x0, waiting for transfers between devices: 45.7 us -> none  [body(): gradient = lax.psum(slice_part, 'cuts')]
  transfers between devices with their start and end apart: 2 -> 1, of which waited for: 2 -> 1; matrix products, arithmetic and copies ran while one was open for 0% -> 0% of each run, Pallas kernels for 0% -> 0%
where the time goes in v2:
time: 903 us
  blocking collectives  794 us (88%)
  waiting for transfers between devices  84.3 us (9%)
  between operations  14.8 us (2%)
    psum x1, blocking collectives, body(): lax.psum(values, ('dp', 'row', 'col'))  649 us
    psum x1, blocking collectives, body(): lax.psum(values, ('dp', 'row'))  129 us
    reduce_scatter x1, waiting for transfers between devices, body(): lax.psum_scatter(gradient_rows(tokens, cotangent, norm_gain), 'dp', scatt...  84.3 us
  transfers between devices with their start and end apart: 1, of which 1 were waited for; matrix products, arithmetic and copies ran while one was open for 0% of the time, Pallas kernels for 0%

profile of v2, /device:TPU:2, one launch (start us, length us, event | category | flops | bytes accessed | tf_op | source)
XLA Modules:
  0.0 902.5 jit_solution(15233530791957234592)
XLA Ops:
  7.2 0.0 copy-start
  7.2 0.0 reduce-scatter.2.cloned.1.call-start
  7.2 1.5 copy-done
  8.8 5.9 convolution_multiply_fusion
  14.7 0.0 copy-start.4
  14.7 0.0 copy-start.2
  14.7 0.0 reduce-scatter.2.cloned.1.call-update
  14.7 84.3 %reduce-scatter.2.cloned.1.call-done = f32[64,1024]{1,0:T(8,128)} async-done(((f32[1024,1024]{1,0:T(8,128)}), f32[64,1024]{1,0:T(8,128)}) %reduce-scatter.2.cloned.1.call-update) | async-done | bytes 262160 | tf_op jit(solution)/shard_map/reduce_scatter | solution.py:34
  99.0 7.2 all-gather
  106.3 0.1 multiply_reduce_fusion.2
  106.4 8.9 psum.21
  115.3 128.7 %psum.22 = f32[1024]{0:T(1024)S(1)} all-reduce(f32[1024]{0:T(1024)S(1)} %get-tuple-element.4), channel_id=1, replica_groups=mesh['cuts'=2,'dp'=16,'row'=4,'col'=4] {'dp','row'}, use_global_device_ids=true, to_apply=%region_5.0 | all-reduce | flops 1024 | bytes 8192 | tf_op jit(solution)/shard_map/psum | solution.py:42
  244.0 0.0 copy-done.4
  244.0 0.0 copy-done.2
  244.0 0.0 copy-start.3
  244.1 0.0 copy-start.1
  244.1 0.8 multiply_reduce_fusion
  244.8 649.3 %psum.23 = f32[]{:T(128)} all-reduce(f32[]{:T(128)} %multiply_reduce_fusion), channel_id=1, replica_groups=mesh['cuts'=2,'dp'=16,'row'=4,'col'=4] {'dp','row','col'}, use_global_device_ids=true, to_apply=%region_7.0 | all-reduce | flops 1 | bytes 8 | tf_op jit(solution)/shard_map/psum | solution.py:43
  894.8 0.8 fusion
  895.7 0.0 copy-done.3
  895.7 0.0 copy-done.1
  (3 shorter events, 0.0 us)
Async XLA Ops:
  7.2 1.6 copy-start
  7.2 91.8 %reduce-scatter.2.cloned.1.call-start = ((), (), s32[]{:S(2)}) async-start(), calls=%async_computation.1 | async-start | bytes 4456448 | tf_op jit(solution)/shard_map/reduce_scatter | solution.py:34
  14.7 229.4 %copy-start.4 = (f32[1,64]{1,0:T(1,128)S(1)}, f32[1,64]{1,0:T(1,128)}, u32[]{:S(2)}) copy-start(f32[1,64]{1,0:T(1,128)} %param.8) | copy-start | bytes 772
  14.7 229.4 %copy-start.2 = (f32[1024]{0:T(1024)S(1)}, f32[1024]{0:T(1024)}, u32[]{:S(2)}) copy-start(f32[1024]{0:T(1024)} %param.9) | copy-start | bytes 12292
  244.0 651.6 %copy-start.3 = (f32[64]{0:T(128)}, f32[64]{0:T(128)S(1)}, u32[]{:S(2)}) copy-start(f32[64]{0:T(128)S(1)} %bitcast_add_fusion) | copy-start | bytes 772
  244.1 651.6 %copy-start.1 = (f32[1024]{0:T(1024)}, f32[1024]{0:T(1024)S(1)}, u32[]{:S(2)}) copy-start(f32[1024]{0:T(1024)S(1)} %multiply_add_fusion) | copy-start | bytes 12292
Sparse Core Ops, SparseCore 0:
  14.8 84.1 reduce-scatter.1
